TPU v7x, 32 devices: a whole 2x2x4 slice. The times are simulated.
32 devices in a mesh: groups: 2 (over y), pipe: 4 (over z), hour: 2 (over x), seg: 2 (over core).
Axes of the slice: x: 2, y: 2, z: 4, core: 2. Of those that a mesh axis runs over, the one named last changes fastest.
Arguments:
- segment_flow: float32 [16, 64, 1024], P(('groups', 'hour'), 'seg', 'pipe'), parts along dimension 0, may hold values from -4 to 4
- linepack: float32 [16, 64, 1024], P(('groups', 'hour'), 'seg', 'pipe'), parts along dimension 0, may hold values from 0.2 to 2.4
- mass_dual: float32 [16, 64, 1024], P(('groups', 'hour'), 'seg', 'pipe'), parts along dimension 0, may hold values from -3 to 3
- momentum_dual: float32 [16, 64, 1024], P(('groups', 'hour'), 'seg', 'pipe'), parts along dimension 0, may hold values from -3 to 3
- contract_dual: float32 [16, 2, 32, 128], P(('groups', 'hour'), 'seg', 'pipe'), parts along dimension 0, may hold values from -3 to 3
- flow_cost: float32 [16, 64, 1024], P(('groups', 'hour'), 'seg', 'pipe'), parts along dimension 0, may hold values from -24 to 24
- injection: float32 [16, 64, 1024], P(('groups', 'hour'), 'seg', 'pipe'), parts along dimension 0, may hold values from -3 to 3
- contract_target: float32 [16, 2, 32, 128], P(('groups', 'hour'), 'seg', 'pipe'), parts along dimension 0, may hold values from 0.4 to 2
- friction_table: float32 [16], replicated, may hold values from 0.3 to 3
- friction_class: int32 [64, 2048], P('seg', ('groups', 'pipe')), parts along dimension 1, may hold values from 0 to 15
- matching: int32 [2048], P('groups'), parts along dimension 0, may hold values from 0 to 1023, as said below
- contract_map: int32 [16, 1024], P(('groups', 'hour')), parts along dimension 0, may hold values from 0 to 127
Outputs:
- flow_final: float32 [16, 64, 1024], P(('groups', 'hour'), 'seg', 'pipe'), parts along dimension 0
- linepack_final: float32 [16, 64, 1024], P(('groups', 'hour'), 'seg', 'pipe'), parts along dimension 0
- mass_dual_final: float32 [16, 64, 1024], P(('groups', 'hour'), 'seg', 'pipe'), parts along dimension 0
- momentum_dual_final: float32 [16, 64, 1024], P(('groups', 'hour'), 'seg', 'pipe'), parts along dimension 0
- contract_dual_final: float32 [16, 2, 32, 128], P(('groups', 'hour'), 'seg', 'pipe'), parts along dimension 0
- primal_weight: float32 [2], P('groups'), parts along dimension 0
There are 2 independent parts, one for each index of `groups`. A program takes and returns all parts, laid end to end along the dimension named above; an argument that names none is the same for every part. Nothing has to cross between parts.
Inputs may be any that keep to these rules, and one draw needn't show every extreme that they name: `matching`: every pipe's inlet is fed by the outlet of exactly one pipe: each number of 0 to 1023 appears once; for any two blocks of 256 consecutive pipes, exactly 64 pipes of the first are fed from outlets of the second.
All inputs are finite; a program needn't handle non-finite values.
Results may differ from a plain program's by a relative error of at most 0.0001.
Values sent between devices are 32-bit elements; how exact they have to be, the bound alone decides.
A program may use at most 64 MiB of HBM per device.

v0:
```python
import math
import jax
import jax.numpy as jnp
from jax import lax
from jax.sharding import PartitionSpec as P

ITERS = 2
FLOW_CAP = 1.5
PACK_CAP = 2.5
STEP_SCALE = 0.25
NORM_EPS = 1e-06


def padded(cells, sides, width):
    for axis, dim in sides:
        count = lax.axis_size(axis)
        ends = count - 1
        head = lax.slice_in_dim(cells, 0, width, axis=dim)
        tail = lax.slice_in_dim(cells, cells.shape[dim] - width, cells.shape[dim], axis=dim)
        cells = jnp.concatenate(
            [
                lax.ppermute(tail, axis, [(i, (i + 1) % count) for i in range(ends)]),
                cells,
                lax.ppermute(head, axis, [((i + 1) % count, i) for i in range(ends)]),
            ],
            axis=dim,
        )
    return cells


def widened_pair(stacked):
    return padded(stacked, (("hour", 1), ("seg", 2)), 1)


def other_half(edge_row, half_index, partner_local):
    gathered = lax.all_gather(edge_row[:, None, :], ("pipe", "seg"), axis=1, tiled=True)
    hour_rows, row_count, row_width = gathered.shape
    seg_count = lax.axis_size("seg")
    picked = gathered.reshape(hour_rows, row_count // seg_count, seg_count, row_width)[
        :, :, half_index, :
    ]
    far_rows = picked.reshape(hour_rows, row_count // seg_count * row_width)
    return jnp.take(far_rows, partner_local, axis=1)


def contract_local(values, contract_rows, class_count):
    hour_rows, seg_rows, pipe_rows = values.shape
    block = math.gcd(pipe_rows, 2048)
    classes = jnp.arange(class_count, dtype=jnp.int32)

    def add_block(block_index, total):
        partial_value = lax.dynamic_slice_in_dim(values, block_index * block, block, 2)
        row_map = lax.dynamic_slice_in_dim(contract_rows, block_index * block, block, 1)
        onehot = (row_map[:, :, None] == classes[None, None, :]).astype(jnp.float32)
        return total + jnp.einsum(
            "hsp,hpc->hsc",
            partial_value,
            onehot,
            precision=lax.Precision.HIGHEST,
            preferred_element_type=jnp.float32,
        )

    return lax.fori_loop(
        0, pipe_rows // block, add_block, jnp.zeros((hour_rows, seg_rows, class_count), jnp.float32)
    )


def spread_local(duals, contract_rows):
    hour_rows, seg_rows, class_count = duals.shape
    pipe_rows = contract_rows.shape[1]
    block = math.gcd(pipe_rows, 2048)
    classes = jnp.arange(class_count, dtype=jnp.int32)

    def fill_block(block_index, result_now):
        row_map = lax.dynamic_slice_in_dim(contract_rows, block_index * block, block, 1)
        onehot = (row_map[:, :, None] == classes[None, None, :]).astype(jnp.float32)
        partial_value = jnp.einsum(
            "hsc,hpc->hsp",
            duals,
            onehot,
            precision=lax.Precision.HIGHEST,
            preferred_element_type=jnp.float32,
        )
        return lax.dynamic_update_slice_in_dim(result_now, partial_value, block_index * block, 2)

    return lax.fori_loop(
        0, pipe_rows // block, fill_block, jnp.zeros((hour_rows, seg_rows, pipe_rows), jnp.float32)
    )


def on_device(
    segment_flow,
    linepack,
    mass_dual,
    momentum_dual,
    contract_dual,
    flow_cost,
    injection,
    contract_target,
    friction_table,
    friction_class,
    matching,
    contract_map,
):
    hour_rows, seg_rows, pipe_rows = segment_flow.shape
    class_count = contract_dual.shape[3]
    pipe_count = lax.axis_size("pipe")
    total_pipes = pipe_rows * pipe_count
    share_scale = class_count / total_pipes
    pipe_start = lax.axis_index("pipe") * pipe_rows
    seg_index = lax.axis_index("seg")
    at_start = seg_index == 0
    at_end = seg_index == lax.axis_size("seg") - 1
    levels = jnp.arange(friction_table.shape[0], dtype=jnp.int32)
    friction = jnp.sum(
        jnp.where(
            friction_class[None] == levels[:, None, None], friction_table[:, None, None], 0.0
        ),
        axis=0,
    )[None]
    inverse = (
        jnp.zeros_like(matching).at[matching].set(jnp.arange(matching.shape[0], dtype=jnp.int32))
    )
    source_local = lax.dynamic_slice_in_dim(matching, pipe_start, pipe_rows)
    target_local = lax.dynamic_slice_in_dim(inverse, pipe_start, pipe_rows)
    contract_now = contract_dual.reshape(hour_rows, contract_dual.shape[2], class_count)
    target_now = contract_target.reshape(hour_rows, contract_target.shape[2], class_count)
    weight = jnp.float32(1.0)
    for iteration in range(ITERS):
        primal_step = STEP_SCALE / weight
        dual_step = STEP_SCALE * weight
        widened = widened_pair(jnp.stack([mass_dual, momentum_dual]))
        last_base = widened[0, 1:-1, -1, :]
        later_hour = widened[0, 2:, 1:-1, :]
        before_seg = widened[1, 1:-1, :-2, :]
        returned = other_half(mass_dual[:, 0, :], 0, target_local)
        last_row = last_base + jnp.where(at_end, returned, 0.0)
        next_seg = jnp.concatenate([mass_dual[:, 1:, :], last_row[:, None, :]], axis=1)
        grad_flow = mass_dual - next_seg + friction * momentum_dual
        hour_spread = spread_local(contract_now, contract_map)
        spread = lax.all_to_all(hour_spread, "pipe", split_axis=2, concat_axis=1, tiled=True)
        grad_pack = mass_dual - later_hour - momentum_dual + before_seg + share_scale * spread
        grad_flow, grad_pack = (grad_flow, grad_pack)
        flow_next = jnp.clip(
            segment_flow - primal_step * (flow_cost - grad_flow), -FLOW_CAP, FLOW_CAP
        )
        pack_next = jnp.clip(linepack + primal_step * grad_pack, 0.0, PACK_CAP)
        flow_bar = 2.0 * flow_next - segment_flow
        pack_bar = 2.0 * pack_next - linepack
        forward_widened = widened_pair(jnp.stack([flow_bar, pack_bar]))
        first_base = forward_widened[0, 1:-1, 0, :]
        earlier = forward_widened[1, :-2, 1:-1, :]
        after_seg = forward_widened[1, 1:-1, 2:, :]
        inflow = other_half(flow_bar[:, -1, :], 1, source_local)
        first_row = first_base + jnp.where(at_start, inflow, 0.0)
        upstream = jnp.concatenate([first_row[:, None, :], flow_bar[:, :-1, :]], axis=1)
        mass_rows = pack_bar - earlier + flow_bar - upstream
        momentum = friction * flow_bar - (pack_bar - after_seg)
        hour_major = lax.all_to_all(pack_bar, "pipe", split_axis=1, concat_axis=2, tiled=True)
        totals = contract_local(hour_major, contract_map, class_count)
        mass_rows, momentum, totals = (mass_rows, momentum, share_scale * totals)
        mass_next = mass_dual + dual_step * (injection - mass_rows)
        momentum_next = momentum_dual - dual_step * momentum
        contract_next = contract_now + dual_step * (target_now - totals)
        primal_sq = jnp.sum((flow_next - segment_flow) ** 2) + jnp.sum((pack_next - linepack) ** 2)
        dual_sq = (
            jnp.sum((mass_next - mass_dual) ** 2)
            + jnp.sum((momentum_next - momentum_dual) ** 2)
            + jnp.sum((contract_next - contract_now) ** 2)
        )
        primal_total, dual_total = lax.psum((primal_sq, dual_sq), ("pipe", "hour", "seg"))
        weight = jnp.sqrt(weight * jnp.sqrt((dual_total + NORM_EPS) / (primal_total + NORM_EPS)))
        segment_flow, linepack = (flow_next, pack_next)
        mass_dual, momentum_dual, contract_now = (mass_next, momentum_next, contract_next)
    return (
        segment_flow,
        linepack,
        mass_dual,
        momentum_dual,
        contract_now.reshape(contract_dual.shape),
        weight.reshape(1),
    )


def solution(mesh):
    return jax.shard_map(
        on_device,
        mesh=mesh,
        in_specs=(
            P(("groups", "hour"), "seg", "pipe"),
            P(("groups", "hour"), "seg", "pipe"),
            P(("groups", "hour"), "seg", "pipe"),
            P(("groups", "hour"), "seg", "pipe"),
            P(("groups", "hour"), "seg", "pipe", None),
            P(("groups", "hour"), "seg", "pipe"),
            P(("groups", "hour"), "seg", "pipe"),
            P(("groups", "hour"), "seg", "pipe", None),
            P(),
            P("seg", ("groups", "pipe")),
            P("groups"),
            P(("groups", "hour"), None),
        ),
        out_specs=(
            P(("groups", "hour"), "seg", "pipe"),
            P(("groups", "hour"), "seg", "pipe"),
            P(("groups", "hour"), "seg", "pipe"),
            P(("groups", "hour"), "seg", "pipe"),
            P(("groups", "hour"), "seg", "pipe", None),
            P("groups"),
        ),
        check_vma=False,
    )
```

profile of v0, /device:TPU:0, one launch (start us, length us, event | category | flops | bytes accessed | tf_op | source)
XLA Modules:
  0.0 255.9 jit_solution(9958504613072737630)
XLA Ops:
  0.6 2.2 fusion.4
  3.7 3.1 %reshape.116 = f32[4,1,8192]{2,1,0:T(1,128)} reshape(f32[1024,4,8]{2,1,0:T(4,128)S(1)} %bitcast.195) | data formatting | bytes 262144
  6.8 6.3 %all-to-all-start = ((f32[4,1,8192]{2,1,0:T(1,128)}), f32[4,1,8192]{2,1,0:T(1,128)S(1)}, u32[]{:S(2)}, u32[]{:S(2)}) async-start(f32[4,1,8192]{2,1,0:T(1,128)} %reshape.116), calls=%async_computation | async-start | bytes 262144 | tf_op jit(solution)/shard_map/all_to_all | solution.py:141
  13.2 1.3 collective-permute-start.1
  14.5 4.5 %collective-permute-start = (f32[2,1,32,256]{3,2,1,0:T(8,128)S(1)}, f32[2,1,32,256]{3,2,1,0:T(8,128)S(1)}, u32[]{:S(2)}, u32[]{:S(2)}) collective-permute-start(f32[2,1,32,256]{3,2,1,0:T(8,128)S(1)} %get-tuple-element.135), channel_id=1, source_target_pairs={{0,2},{1,3},{4,6},{5,7},{8,10},{9,11},{12,14},{13,15},{16,18},{17,... | collective-permute-start | bytes 196616 | tf_op jit(solution)/shard_map/ppermute | solution.py:22
  19.1 14.6 %all_gather.12 = f32[4,8,256]{2,0,1:T(4,128)S(1)} all-gather(f32[4,1,256]{2,0,1:T(4,128)S(1)} %copy.255), channel_id=1, replica_groups=mesh['groups'=2,'pipe'=4,'hour'=2,'seg'=2] {'pipe','seg'}, dimensions={1}, use_global_device_ids=true | all-gather | bytes 36864 | tf_op jit(solution)/shard_map/all_gather | solution.py:36
  33.9 4.3 %scatter_custom_fusion = s32[1024]{0:T(1024)S(1)} fusion(s32[1024]{0:T(1024)S(1)} %compare_select_fusion, s32[1024]{0:T(1024)S(1)} %iota.14, s32[]{:T(128)} %constant.26.clone.1), kind=kCustom, calls=%fused_computation.140 | custom fusion | bytes 4100 | tf_op jit(solution)/shard_map/scatter | solution.py:122
  40.3 2.2 collective-permute-start.3
  42.7 1.3 collective-permute-start.2
  44.6 1.5 collective-permute-done.2
  47.8 2.5 reshape.117
  50.4 1.8 broadcast_multiply_fusion.1
  52.2 1.9 copy.145
  54.1 1.2 multiply_reduce_fusion.4
  57.2 1.4 collective-permute-start.5
  58.7 4.5 %collective-permute-start.4 = (f32[2,1,32,256]{3,2,1,0:T(8,128)S(1)}, f32[2,1,32,256]{3,2,1,0:T(8,128)S(1)}, u32[]{:S(2)}, u32[]{:S(2)}) collective-permute-start(f32[2,1,32,256]{3,2,1,0:T(8,128)S(1)} %get-tuple-element.131), channel_id=1, source_target_pairs={{0,2},{1,3},{4,6},{5,7},{8,10},{9,11},{12,14},{13,15},{16,18},{17,... | collective-permute-start | bytes 196616 | tf_op jit(solution)/shard_map/ppermute | solution.py:22
  63.3 14.0 %all_gather.13 = f32[4,8,256]{2,0,1:T(4,128)S(1)} all-gather(f32[4,1,256]{2,0,1:T(4,128)S(1)} %slice.182), channel_id=1, replica_groups=mesh['groups'=2,'pipe'=4,'hour'=2,'seg'=2] {'pipe','seg'}, dimensions={1}, use_global_device_ids=true | all-gather | bytes 36864 | tf_op jit(solution)/shard_map/all_gather | solution.py:36
  78.7 2.2 collective-permute-start.6
  81.0 1.5 collective-permute-start.7
  82.7 1.4 collective-permute-done.7
  84.0 2.0 multiply_reduce_fusion.7
  86.2 1.3 collective-permute-start.9
  87.5 4.5 %collective-permute-start.8 = (f32[2,1,32,256]{3,2,1,0:T(8,128)S(1)}, f32[2,1,32,256]{3,2,1,0:T(8,128)S(1)}, u32[]{:S(2)}, u32[]{:S(2)}) collective-permute-start(f32[2,1,32,256]{3,2,1,0:T(8,128)S(1)} %get-tuple-element.127), channel_id=1, source_target_pairs={{0,2},{1,3},{4,6},{5,7},{8,10},{9,11},{12,14},{13,15},{16,18},{17,... | collective-permute-start | bytes 196616 | tf_op jit(solution)/shard_map/ppermute | solution.py:22
  92.0 4.5 %all-to-all-start.1 = ((f32[4,32,256]{2,0,1:T(4,128)}), f32[4,32,256]{2,0,1:T(4,128)S(1)}, u32[]{:S(2)}, u32[]{:S(2)}) async-start(f32[4,32,256]{2,0,1:T(4,128)} %multiply_subtract_fusion.3), calls=%async_computation.1 | async-start | bytes 262144 | tf_op jit(solution)/shard_map/all_to_all | solution.py:159
  98.5 14.6 %all_gather.14 = f32[4,8,256]{2,0,1:T(4,128)S(1)} all-gather(f32[4,1,256]{2,0,1:T(4,128)S(1)} %slice.191), channel_id=1, replica_groups=mesh['groups'=2,'pipe'=4,'hour'=2,'seg'=2] {'pipe','seg'}, dimensions={1}, use_global_device_ids=true | all-gather | bytes 36864 | tf_op jit(solution)/shard_map/all_gather | solution.py:36
  113.3 1.3 gather_fusion.2
  116.3 2.2 collective-permute-start.11
  119.3 1.3 collective-permute-start.10
  120.7 2.2 fusion.73
  122.9 1.8 fusion.1
  125.6 3.1 %reshape.118 = f32[4,1,8192]{2,1,0:T(1,128)} reshape(f32[1024,4,8]{2,1,0:T(4,128)S(1)} %bitcast.197) | data formatting | bytes 262144
  128.7 4.5 %all-to-all-start.2 = ((f32[4,1,8192]{2,1,0:T(1,128)}), f32[4,1,8192]{2,1,0:T(1,128)S(1)}, u32[]{:S(2)}, u32[]{:S(2)}) async-start(f32[4,1,8192]{2,1,0:T(1,128)} %reshape.118), calls=%async_computation.2 | async-start | bytes 262144 | tf_op jit(solution)/shard_map/all_to_all | solution.py:141
  133.2 1.1 fusion.31
  135.1 33.5 %all-reduce.1 = (f32[]{:T(128)}, f32[]{:T(128)}) all-reduce(f32[]{:T(128)S(6)} %add.153, f32[]{:T(128)S(6)} %add.155), channel_id=1, replica_groups=mesh['groups'=2,'pipe'=4,'hour'=2,'seg'=2] {'pipe','hour','seg'}, use_global_device_ids=true, to_apply=%region_5.7 | all-reduce | flops 2 | bytes 16 | tf_op jit(solution)/shard_map/psum | solution.py:171
  170.1 1.0 reduce.1
  171.0 2.5 reshape.119
  173.6 1.8 broadcast_multiply_fusion
  175.4 1.9 copy.175
  180.0 1.3 collective-permute-start.13
  181.3 4.5 %collective-permute-start.12 = (f32[2,1,32,256]{3,2,1,0:T(8,128)S(1)}, f32[2,1,32,256]{3,2,1,0:T(8,128)S(1)}, u32[]{:S(2)}, u32[]{:S(2)}) collective-permute-start(f32[2,1,32,256]{3,2,1,0:T(8,128)S(1)} %get-tuple-element.123), channel_id=1, source_target_pairs={{0,2},{1,3},{4,6},{5,7},{8,10},{9,11},{12,14},{13,15},{16,18},{17,... | collective-permute-start | bytes 196616 | tf_op jit(solution)/shard_map/ppermute | solution.py:22
  187.2 3.5 %all-to-all-start.3 = ((f32[4,32,256]{2,0,1:T(4,128)}), f32[4,32,256]{2,0,1:T(4,128)S(1)}, u32[]{:S(2)}, u32[]{:S(2)}) async-start(f32[4,32,256]{2,0,1:T(4,128)} %multiply_subtract_fusion.1), calls=%async_computation.3 | async-start | bytes 262144 | tf_op jit(solution)/shard_map/all_to_all | solution.py:159
  190.7 14.6 %all_gather.15 = f32[4,8,256]{2,0,1:T(4,128)S(1)} all-gather(f32[4,1,256]{2,0,1:T(4,128)S(1)} %slice.198), channel_id=1, replica_groups=mesh['groups'=2,'pipe'=4,'hour'=2,'seg'=2] {'pipe','seg'}, dimensions={1}, use_global_device_ids=true | all-gather | bytes 36864 | tf_op jit(solution)/shard_map/all_gather | solution.py:36
  207.9 1.3 collective-permute-start.15
  209.4 3.0 %collective-permute-start.14 = (f32[2,6,1,256]{1,3,2,0:T(8,128)S(1)}, f32[2,6,1,256]{1,3,2,0:T(8,128)S(1)}, u32[]{:S(2)}, u32[]{:S(2)}) collective-permute-start(f32[2,6,1,256]{1,3,2,0:T(8,128)S(1)} %copy.201), channel_id=1, source_target_pairs={{0,1},{2,3},{4,5},{6,7},{8,9},{10,11},{12,13},{14,15},{16,17},{18,... | collective-permute-start | bytes 36872 | tf_op jit(solution)/shard_map/ppermute | solution.py:22
  212.4 1.1 collective-permute-done.14
  213.8 1.8 multiply_reduce_fusion.2
  217.6 2.4 multiply_reduce_fusion.8
  221.4 32.0 %all-reduce = (f32[]{:T(128)}, f32[]{:T(128)}) all-reduce(f32[]{:T(128)S(6)} %add.167, f32[]{:T(128)S(6)} %add.169), channel_id=1, replica_groups=mesh['groups'=2,'pipe'=4,'hour'=2,'seg'=2] {'pipe','hour','seg'}, use_global_device_ids=true, to_apply=%region_12.14 | all-reduce | flops 2 | bytes 16 | tf_op jit(solution)/shard_map/psum | solution.py:171
  (135 shorter events, 19.3 us)
Async XLA Ops:
  2.8 10.3 %copy-start = (f32[4,32,256]{2,1,0:T(8,128)S(1)}, f32[4,32,256]{2,1,0:T(8,128)}, u32[]{:S(2)}) copy-start(f32[4,32,256]{2,1,0:T(8,128)} %param.16) | copy-start | bytes 393220
  2.8 10.3 %copy-start.1 = (f32[4,32,256]{2,1,0:T(8,128)S(1)}, f32[4,32,256]{2,1,0:T(8,128)}, u32[]{:S(2)}) copy-start(f32[4,32,256]{2,1,0:T(8,128)} %param.17) | copy-start | bytes 393220
  3.7 30.2 %copy-start.12 = (s32[1024]{0:T(1024)S(1)}, s32[1024]{0:T(1024)}, u32[]{:S(2)}) copy-start(s32[1024]{0:T(1024)} %param.24) | copy-start | bytes 12292
  3.7 35.3 %copy-start.11 = (s32[32,256]{1,0:T(8,128)S(1)}, s32[32,256]{1,0:T(8,128)}, u32[]{:S(2)}) copy-start(s32[32,256]{1,0:T(8,128)} %param.23) | copy-start | bytes 98308
  3.7 35.3 %copy-start.13 = (f32[16]{0:T(128)S(1)}, f32[16]{0:T(128)}, u32[]{:S(2)}) copy-start(f32[16]{0:T(128)} %param.22) | copy-start | bytes 196
  6.8 39.5 %all-to-all-start = ((f32[4,1,8192]{2,1,0:T(1,128)}), f32[4,1,8192]{2,1,0:T(1,128)S(1)}, u32[]{:S(2)}, u32[]{:S(2)}) async-start(f32[4,1,8192]{2,1,0:T(1,128)} %reshape.116), calls=%async_computation | async-start | bytes 262144 | tf_op jit(solution)/shard_map/all_to_all | solution.py:141
  13.2 26.8 %collective-permute-start.1 = (f32[2,1,32,256]{3,2,1,0:T(8,128)S(1)}, f32[2,1,32,256]{3,2,1,0:T(8,128)S(1)}, u32[]{:S(2)}, u32[]{:S(2)}) collective-permute-start(f32[2,1,32,256]{3,2,1,0:T(8,128)S(1)} %get-tuple-element.136), channel_id=1, source_target_pairs={{2,0},{3,1},{6,4},{7,5},{10,8},{11,9},{14,12},{15,13},{18,16},{19,... | collective-permute-start | bytes 196616 | tf_op jit(solution)/shard_map/ppermute | solution.py:24
  14.5 25.5 %collective-permute-start = (f32[2,1,32,256]{3,2,1,0:T(8,128)S(1)}, f32[2,1,32,256]{3,2,1,0:T(8,128)S(1)}, u32[]{:S(2)}, u32[]{:S(2)}) collective-permute-start(f32[2,1,32,256]{3,2,1,0:T(8,128)S(1)} %get-tuple-element.135), channel_id=1, source_target_pairs={{0,2},{1,3},{4,6},{5,7},{8,10},{9,11},{12,14},{13,15},{16,18},{17,... | collective-permute-start | bytes 196616 | tf_op jit(solution)/shard_map/ppermute | solution.py:22
  40.3 13.8 %collective-permute-start.3 = (f32[2,6,1,256]{3,1,2,0:T(8,128)S(1)}, f32[2,6,1,256]{3,1,2,0:T(8,128)S(1)}, u32[]{:S(2)}, u32[]{:S(2)}) collective-permute-start(f32[2,6,1,256]{3,1,2,0:T(8,128)S(1)} %slice.177), channel_id=1, source_target_pairs={{0,1},{2,3},{4,5},{6,7},{8,9},{10,11},{12,13},{14,15},{16,17},{18,... | collective-permute-start | bytes 36872 | tf_op jit(solution)/shard_map/ppermute | solution.py:22
  42.7 3.4 %collective-permute-start.2 = (f32[2,6,1,256]{1,3,2,0:T(8,128)S(1)}, f32[2,6,1,256]{1,3,2,0:T(8,128)S(1)}, u32[]{:S(2)}, u32[]{:S(2)}) collective-permute-start(f32[2,6,1,256]{1,3,2,0:T(8,128)S(1)} %copy.191), channel_id=1, source_target_pairs={{1,0},{3,2},{5,4},{7,6},{9,8},{11,10},{13,12},{15,14},{17,16},{19,... | collective-permute-start | bytes 36872 | tf_op jit(solution)/shard_map/ppermute | solution.py:24
  52.1 1.9 copy-start.2
  52.2 2.0 copy-start.3
  52.2 2.0 copy-start.4
  52.2 2.0 copy-start.8
  52.2 2.0 copy-start.9
  57.2 26.8 %copy-start.6 = (f32[4,32,256]{2,1,0:T(8,128)S(1)}, f32[4,32,256]{2,1,0:T(8,128)}, u32[]{:S(2)}) copy-start(f32[4,32,256]{2,1,0:T(8,128)} %param.20) | copy-start | bytes 393220
  57.2 21.0 %collective-permute-start.5 = (f32[2,1,32,256]{3,2,1,0:T(8,128)S(1)}, f32[2,1,32,256]{3,2,1,0:T(8,128)S(1)}, u32[]{:S(2)}, u32[]{:S(2)}) collective-permute-start(f32[2,1,32,256]{3,2,1,0:T(8,128)S(1)} %get-tuple-element.132), channel_id=1, source_target_pairs={{2,0},{3,1},{6,4},{7,5},{10,8},{11,9},{14,12},{15,13},{18,16},{19,... | collective-permute-start | bytes 196616 | tf_op jit(solution)/shard_map/ppermute | solution.py:24
  58.7 19.6 %collective-permute-start.4 = (f32[2,1,32,256]{3,2,1,0:T(8,128)S(1)}, f32[2,1,32,256]{3,2,1,0:T(8,128)S(1)}, u32[]{:S(2)}, u32[]{:S(2)}) collective-permute-start(f32[2,1,32,256]{3,2,1,0:T(8,128)S(1)} %get-tuple-element.131), channel_id=1, source_target_pairs={{0,2},{1,3},{4,6},{5,7},{8,10},{9,11},{12,14},{13,15},{16,18},{17,... | collective-permute-start | bytes 196616 | tf_op jit(solution)/shard_map/ppermute | solution.py:22
  78.7 3.7 %collective-permute-start.6 = (f32[2,6,1,256]{1,3,2,0:T(8,128)S(1)}, f32[2,6,1,256]{1,3,2,0:T(8,128)S(1)}, u32[]{:S(2)}, u32[]{:S(2)}) collective-permute-start(f32[2,6,1,256]{1,3,2,0:T(8,128)S(1)} %copy.195), channel_id=1, source_target_pairs={{0,1},{2,3},{4,5},{6,7},{8,9},{10,11},{12,13},{14,15},{16,17},{18,... | collective-permute-start | bytes 36872 | tf_op jit(solution)/shard_map/ppermute | solution.py:22
  81.0 3.1 %collective-permute-start.7 = (f32[2,6,1,256]{3,1,2,0:T(8,128)S(1)}, f32[2,6,1,256]{3,1,2,0:T(8,128)S(1)}, u32[]{:S(2)}, u32[]{:S(2)}) collective-permute-start(f32[2,6,1,256]{3,1,2,0:T(8,128)S(1)} %slice.185), channel_id=1, source_target_pairs={{1,0},{3,2},{5,4},{7,6},{9,8},{11,10},{13,12},{15,14},{17,16},{19,... | collective-permute-start | bytes 36872 | tf_op jit(solution)/shard_map/ppermute | solution.py:24
  86.1 34.6 %copy-start.14 = (f32[4,1,8,128]{3,2,1,0:T(8,128)S(1)}, f32[4,1,8,128]{3,2,1,0:T(8,128)}, u32[]{:S(2)}) copy-start(f32[4,1,8,128]{3,2,1,0:T(8,128)} %param.18) | copy-start | bytes 49156
  86.1 34.6 %copy-start.15 = (s32[4,1024]{1,0:T(4,128)S(1)}, s32[4,1024]{1,0:T(4,128)}, u32[]{:S(2)}) copy-start(s32[4,1024]{1,0:T(4,128)} %param.25) | copy-start | bytes 49156
  86.1 34.6 %copy-start.16 = (f32[4,1,8,128]{3,2,1,0:T(8,128)S(1)}, f32[4,1,8,128]{3,2,1,0:T(8,128)}, u32[]{:S(2)}) copy-start(f32[4,1,8,128]{3,2,1,0:T(8,128)} %param.21) | copy-start | bytes 49156
  86.2 29.8 %collective-permute-start.9 = (f32[2,1,32,256]{3,2,1,0:T(8,128)S(1)}, f32[2,1,32,256]{3,2,1,0:T(8,128)S(1)}, u32[]{:S(2)}, u32[]{:S(2)}) collective-permute-start(f32[2,1,32,256]{3,2,1,0:T(8,128)S(1)} %get-tuple-element.128), channel_id=1, source_target_pairs={{2,0},{3,1},{6,4},{7,5},{10,8},{11,9},{14,12},{15,13},{18,16},{19,... | collective-permute-start | bytes 196616 | tf_op jit(solution)/shard_map/ppermute | solution.py:24
  87.5 28.5 %collective-permute-start.8 = (f32[2,1,32,256]{3,2,1,0:T(8,128)S(1)}, f32[2,1,32,256]{3,2,1,0:T(8,128)S(1)}, u32[]{:S(2)}, u32[]{:S(2)}) collective-permute-start(f32[2,1,32,256]{3,2,1,0:T(8,128)S(1)} %get-tuple-element.127), channel_id=1, source_target_pairs={{0,2},{1,3},{4,6},{5,7},{8,10},{9,11},{12,14},{13,15},{16,18},{17,... | collective-permute-start | bytes 196616 | tf_op jit(solution)/shard_map/ppermute | solution.py:22
  92.0 28.6 %all-to-all-start.1 = ((f32[4,32,256]{2,0,1:T(4,128)}), f32[4,32,256]{2,0,1:T(4,128)S(1)}, u32[]{:S(2)}, u32[]{:S(2)}) async-start(f32[4,32,256]{2,0,1:T(4,128)} %multiply_subtract_fusion.3), calls=%async_computation.1 | async-start | bytes 262144 | tf_op jit(solution)/shard_map/all_to_all | solution.py:159
  116.3 61.0 %collective-permute-start.11 = (f32[2,6,1,256]{3,1,2,0:T(8,128)S(1)}, f32[2,6,1,256]{3,1,2,0:T(8,128)S(1)}, u32[]{:S(2)}, u32[]{:S(2)}) collective-permute-start(f32[2,6,1,256]{3,1,2,0:T(8,128)S(1)} %slice.193), channel_id=1, source_target_pairs={{0,1},{2,3},{4,5},{6,7},{8,9},{10,11},{12,13},{14,15},{16,17},{18,... | collective-permute-start | bytes 36872 | tf_op jit(solution)/shard_map/ppermute | solution.py:22
  119.3 13.9 %collective-permute-start.10 = (f32[2,6,1,256]{1,3,2,0:T(8,128)}, f32[2,6,1,256]{1,3,2,0:T(8,128)}, u32[]{:S(2)}, u32[]{:S(2)}) collective-permute-start(f32[2,6,1,256]{1,3,2,0:T(8,128)} %copy.197), channel_id=1, source_target_pairs={{1,0},{3,2},{5,4},{7,6},{9,8},{11,10},{13,12},{15,14},{17,16},{19,... | collective-permute-start | bytes 36872 | tf_op jit(solution)/shard_map/ppermute | solution.py:24
  128.7 41.3 %all-to-all-start.2 = ((f32[4,1,8192]{2,1,0:T(1,128)}), f32[4,1,8192]{2,1,0:T(1,128)S(1)}, u32[]{:S(2)}, u32[]{:S(2)}) async-start(f32[4,1,8192]{2,1,0:T(1,128)} %reshape.118), calls=%async_computation.2 | async-start | bytes 262144 | tf_op jit(solution)/shard_map/all_to_all | solution.py:141
  175.4 1.9 copy-start.5
  175.4 1.9 copy-start.10
  180.0 27.6 %collective-permute-start.13 = (f32[2,1,32,256]{3,2,1,0:T(8,128)S(1)}, f32[2,1,32,256]{3,2,1,0:T(8,128)S(1)}, u32[]{:S(2)}, u32[]{:S(2)}) collective-permute-start(f32[2,1,32,256]{3,2,1,0:T(8,128)S(1)} %get-tuple-element.124), channel_id=1, source_target_pairs={{2,0},{3,1},{6,4},{7,5},{10,8},{11,9},{14,12},{15,13},{18,16},{19,... | collective-permute-start | bytes 196616 | tf_op jit(solution)/shard_map/ppermute | solution.py:24
  181.3 26.3 %collective-permute-start.12 = (f32[2,1,32,256]{3,2,1,0:T(8,128)S(1)}, f32[2,1,32,256]{3,2,1,0:T(8,128)S(1)}, u32[]{:S(2)}, u32[]{:S(2)}) collective-permute-start(f32[2,1,32,256]{3,2,1,0:T(8,128)S(1)} %get-tuple-element.123), channel_id=1, source_target_pairs={{0,2},{1,3},{4,6},{5,7},{8,10},{9,11},{12,14},{13,15},{16,18},{17,... | collective-permute-start | bytes 196616 | tf_op jit(solution)/shard_map/ppermute | solution.py:22
  187.2 26.6 %copy-start.7 = (f32[4,32,256]{2,1,0:T(8,128)S(1)}, f32[4,32,256]{2,1,0:T(8,128)}, u32[]{:S(2)}) copy-start(f32[4,32,256]{2,1,0:T(8,128)} %param.20) | copy-start | bytes 393220
  187.2 30.4 %all-to-all-start.3 = ((f32[4,32,256]{2,0,1:T(4,128)}), f32[4,32,256]{2,0,1:T(4,128)S(1)}, u32[]{:S(2)}, u32[]{:S(2)}) async-start(f32[4,32,256]{2,0,1:T(4,128)} %multiply_subtract_fusion.1), calls=%async_computation.3 | async-start | bytes 262144 | tf_op jit(solution)/shard_map/all_to_all | solution.py:159
  207.9 5.8 %collective-permute-start.15 = (f32[2,6,1,256]{3,1,2,0:T(8,128)S(1)}, f32[2,6,1,256]{3,1,2,0:T(8,128)S(1)}, u32[]{:S(2)}, u32[]{:S(2)}) collective-permute-start(f32[2,6,1,256]{3,1,2,0:T(8,128)S(1)} %slice.201), channel_id=1, source_target_pairs={{1,0},{3,2},{5,4},{7,6},{9,8},{11,10},{13,12},{15,14},{17,16},{19,... | collective-permute-start | bytes 36872 | tf_op jit(solution)/shard_map/ppermute | solution.py:24
  209.4 4.2 %collective-permute-start.14 = (f32[2,6,1,256]{1,3,2,0:T(8,128)S(1)}, f32[2,6,1,256]{1,3,2,0:T(8,128)S(1)}, u32[]{:S(2)}, u32[]{:S(2)}) collective-permute-start(f32[2,6,1,256]{1,3,2,0:T(8,128)S(1)} %copy.201), channel_id=1, source_target_pairs={{0,1},{2,3},{4,5},{6,7},{8,9},{10,11},{12,13},{14,15},{16,17},{18,... | collective-permute-start | bytes 36872 | tf_op jit(solution)/shard_map/ppermute | solution.py:22
where the time goes:
time: 257 us; the launch traced here: 256 us
  blocking collectives  123 us (48%)
  starting transfers between devices  57.3 us (22%)
  local copies, waits for them, and re-layouts  34.9 us (14%)
  other arithmetic  15.8 us (6%)
  between operations  12.1 us (5%)
  matrix products  8.66 us (3%)
  waiting for transfers between devices  3.97 us (2%)
    psum x2, blocking collectives, on_device(): lax.psum((primal_sq, dual_sq), ('pipe', 'hour', 'seg'))  65.5 us
    all_gather x4, blocking collectives, other_half(): lax.all_gather(edge_row[:, None, :], ('pipe', 'seg'), axis=1, tiled=True)  57.8 us
    ppermute x8, starting transfers between devices, padded(): lax.ppermute(tail, axis, [(i, (i + 1) % count) for i in range(ends)])  27.9 us
    unnamed x55, local copies, waits for them, and re-layouts  17 us
    all_to_all x2, starting transfers between devices, on_device(): lax.all_to_all(hour_spread, 'pipe', split_axis=2, concat_axis=1, tiled=True)  10.8 us
    ppermute x8, starting transfers between devices, padded(): lax.ppermute(head, axis, [((i + 1) % count, i) for i in range(ends)])  10.6 us
    all_to_all x2, starting transfers between devices, on_device(): lax.all_to_all(pack_bar, 'pipe', split_axis=1, concat_axis=2, tiled=True)  7.96 us
  transfers between devices with their start and end apart: 20, of which 3 were waited for; matrix products, arithmetic and copies ran while one was open for 16% of the time, Pallas kernels for 0%

commit v1 on v0

--- a/solution.py
+++ b/solution.py
@@ -33,7 +33,29 @@
 
 
 def other_half(edge_row, half_index, partner_local):
-    gathered = lax.all_gather(edge_row[:, None, :], ("pipe", "seg"), axis=1, tiled=True)
+    array = edge_row[:, None, :]
+    size, index, rows = (
+        lax.axis_size(("pipe", "seg")),
+        lax.axis_index(("pipe", "seg")),
+        array.shape[1],
+    )
+    right = [(i_2, (i_2 + 1) % size) for i_2 in range(size)]
+    downward = [(i_2, (i_2 - 1) % size) for i_2 in range(size)]
+    filled = jnp.zeros((*array.shape[:1], size * rows, *array.shape[1 + 1 :]), array.dtype)
+    filled = lax.dynamic_update_slice_in_dim(filled, array, index * rows, axis=1)
+    from_left = from_right = array
+    halfway = size // 2
+    for step in range(1, halfway + 1):
+        from_left = lax.ppermute(from_left, ("pipe", "seg"), right)
+        filled = lax.dynamic_update_slice_in_dim(
+            filled, from_left, (index - step) % size * rows, axis=1
+        )
+        if step < size - halfway:
+            from_right = lax.ppermute(from_right, ("pipe", "seg"), downward)
+            filled = lax.dynamic_update_slice_in_dim(
+                filled, from_right, (index + step) % size * rows, axis=1
+            )
+    gathered = filled
     hour_rows, row_count, row_width = gathered.shape
     seg_count = lax.axis_size("seg")
     picked = gathered.reshape(hour_rows, row_count // seg_count, seg_count, row_width)[

time: 257 us -> 267 us (1.039)
  blocking collectives: 123 us -> 64.1 us
  starting transfers between devices: 57.3 us -> 92.7 us
  waiting for transfers between devices: 3.97 us -> 33.7 us
  local copies, waits for them, and re-layouts: 34.9 us -> 37.7 us
    all_gather x4 -> x0, blocking collectives: 57.8 us -> none  [other_half(): lax.all_gather(edge_row[:, None, :], ('pipe', 'seg'), axis=1, tiled=True)]
    ppermute x0 -> x28, starting transfers between devices: none -> 43.6 us  [the longest x12 42.4 us: other_half(): from_right = lax.ppermute(from_right, ('pipe', 'seg'), downward)]
    ppermute x0 -> x28, waiting for transfers between devices: none -> 29.6 us  [the longest x16 29.2 us: other_half(): from_left = lax.ppermute(from_left, ('pipe', 'seg'), right)]
    all_to_all x2, starting transfers between devices: 10.8 us -> 6.9 us  [on_device(): lax.all_to_all(hour_spread, 'pipe', split_axis=2, concat_axis=1, tiled=True)]
    unnamed x55 -> x48, local copies, waits for them, and re-layouts: 17 us -> 17 us
  transfers between devices with their start and end apart: 20 -> 48, of which waited for: 3 -> 15; matrix products, arithmetic and copies ran while one was open for 16% -> 21% of each run, Pallas kernels for 0% -> 0%
where the time goes in v1:
time: 267 us; the launch traced here: 266 us
  starting transfers between devices  92.7 us (35%)
  blocking collectives  64.1 us (24%)
  local copies, waits for them, and re-layouts  37.7 us (14%)
  waiting for transfers between devices  33.7 us (13%)
  other arithmetic  16.4 us (6%)
  between operations  12.2 us (5%)
  matrix products  8.91 us (3%)
    psum x2, blocking collectives, on_device(): lax.psum((primal_sq, dual_sq), ('pipe', 'hour', 'seg'))  64.1 us
    ppermute x12, starting transfers between devices, other_half(): from_right = lax.ppermute(from_right, ('pipe', 'seg'), downward)  42.4 us
    ppermute x16, waiting for transfers between devices, other_half(): from_left = lax.ppermute(from_left, ('pipe', 'seg'), right)  29.2 us
    ppermute x8, starting transfers between devices, padded(): lax.ppermute(tail, axis, [(i, (i + 1) % count) for i in range(ends)])  25.3 us
    unnamed x48, local copies, waits for them, and re-layouts  17 us
    ppermute x8, starting transfers between devices, padded(): lax.ppermute(head, axis, [((i + 1) % count, i) for i in range(ends)])  10.3 us
    all_to_all x2, starting transfers between devices, on_device(): lax.all_to_all(hour_spread, 'pipe', split_axis=2, concat_axis=1, tiled=True)  6.9 us
    all_to_all x2, starting transfers between devices, on_device(): lax.all_to_all(pack_bar, 'pipe', split_axis=1, concat_axis=2, tiled=True)  6.66 us
  transfers between devices with their start and end apart: 48, of which 15 were waited for; matrix products, arithmetic and copies ran while one was open for 21% of the time, Pallas kernels for 0%

profile of v1, /device:TPU:0, one launch (start us, length us, event | category | flops | bytes accessed | tf_op | source)
XLA Modules:
  0.0 265.7 jit_solution(11032236407211072517)
XLA Ops:
  1.8 4.0 %collective-permute-start.4 = (f32[4,1,256]{2,1,0:T(1,128)S(1)}, f32[4,1,256]{2,1,0:T(1,128)S(1)}, u32[]{:S(2)}, u32[]{:S(2)}) collective-permute-start(f32[4,1,256]{2,1,0:T(1,128)S(1)} %slice.129), channel_id=1, source_target_pairs={{0,13},{1,0},{4,1},{5,4},{8,5},{9,8},{12,9},{13,12},{2,15},{3,2},{... | collective-permute-start | bytes 12296 | tf_op jit(solution)/shard_map/ppermute | solution.py:54
  5.9 2.2 fusion.4
  9.0 3.1 %reshape.116 = f32[4,1,8192]{2,1,0:T(1,128)} reshape(f32[1024,4,8]{2,1,0:T(4,128)S(1)} %bitcast.195) | data formatting | bytes 262144
  12.1 3.6 %all-to-all-start = ((f32[4,1,8192]{2,1,0:T(1,128)}), f32[4,1,8192]{2,1,0:T(1,128)S(1)}, u32[]{:S(2)}, u32[]{:S(2)}) async-start(f32[4,1,8192]{2,1,0:T(1,128)} %reshape.116), calls=%async_computation | async-start | bytes 262144 | tf_op jit(solution)/shard_map/all_to_all | solution.py:163
  16.9 4.5 %collective-permute-start = (f32[2,1,32,256]{3,2,1,0:T(8,128)S(1)}, f32[2,1,32,256]{3,2,1,0:T(8,128)S(1)}, u32[]{:S(2)}, u32[]{:S(2)}) collective-permute-start(f32[2,1,32,256]{3,2,1,0:T(8,128)S(1)} %get-tuple-element.141), channel_id=1, source_target_pairs={{0,2},{1,3},{4,6},{5,7},{8,10},{9,11},{12,14},{13,15},{16,18},{17,... | collective-permute-start | bytes 196616 | tf_op jit(solution)/shard_map/ppermute | solution.py:22
  21.7 4.3 %scatter_custom_fusion = s32[1024]{0:T(1024)S(1)} fusion(s32[1024]{0:T(1024)S(1)} %compare_select_fusion, s32[1024]{0:T(1024)S(1)} %iota.14, s32[]{:T(128)} %constant.152.clone.1), kind=kCustom, calls=%fused_computation.172 | custom fusion | bytes 4100 | tf_op jit(solution)/shard_map/scatter | solution.py:144
  27.1 3.5 %collective-permute-start.6 = (f32[4,1,256]{2,1,0:T(1,128)S(1)}, f32[4,1,256]{2,1,0:T(1,128)S(1)}, u32[]{:S(2)}, u32[]{:S(2)}) collective-permute-start(f32[4,1,256]{2,1,0:T(1,128)S(1)} %collective-permute-done.4), channel_id=1, source_target_pairs={{0,13},{1,0},{4,1},{5,4},{8,5},{9,8},{12,9},{13,12},{2,15},{3,2},{... | collective-permute-start | bytes 12296 | tf_op jit(solution)/shard_map/ppermute | solution.py:54
  32.0 3.5 %collective-permute-start.8 = (f32[4,1,256]{2,1,0:T(1,128)S(1)}, f32[4,1,256]{2,1,0:T(1,128)S(1)}, u32[]{:S(2)}, u32[]{:S(2)}) collective-permute-start(f32[4,1,256]{2,1,0:T(1,128)S(1)} %collective-permute-done.6), channel_id=1, source_target_pairs={{0,13},{1,0},{4,1},{5,4},{8,5},{9,8},{12,9},{13,12},{2,15},{3,2},{... | collective-permute-start | bytes 12296 | tf_op jit(solution)/shard_map/ppermute | solution.py:54
  36.8 4.8 %collective-permute-done.9 = f32[4,1,256]{2,1,0:T(1,128)S(1)} collective-permute-done((f32[4,1,256]{2,1,0:T(1,128)S(1)}, f32[4,1,256]{2,1,0:T(1,128)S(1)}, u32[]{:S(2)}, u32[]{:S(2)}) %collective-permute-start.9) | collective-permute-done | bytes 4128 | tf_op jit(solution)/shard_map/ppermute | solution.py:49
  46.3 1.5 collective-permute-done.2
  49.5 2.5 reshape.117
  52.0 1.8 broadcast_multiply_fusion.1
  53.9 1.9 copy.242
  57.4 3.4 %collective-permute-start.15 = (f32[4,1,256]{2,0,1:T(4,128)S(1)}, f32[4,1,256]{2,0,1:T(4,128)S(1)}, u32[]{:S(2)}, u32[]{:S(2)}) collective-permute-start(f32[4,1,256]{2,0,1:T(4,128)S(1)} %get-tuple-element.147), channel_id=1, source_target_pairs={{0,13},{1,0},{4,1},{5,4},{8,5},{9,8},{12,9},{13,12},{2,15},{3,2},{... | collective-permute-start | bytes 12296 | tf_op jit(solution)/shard_map/ppermute | solution.py:54
  61.6 3.3 %all-to-all-start.1 = ((f32[4,32,256]{2,0,1:T(4,128)}), f32[4,32,256]{2,0,1:T(4,128)S(1)}, u32[]{:S(2)}, u32[]{:S(2)}) async-start(f32[4,32,256]{2,0,1:T(4,128)} %multiply_subtract_fusion.3), calls=%async_computation.1 | async-start | bytes 262144 | tf_op jit(solution)/shard_map/all_to_all | solution.py:181
  67.2 4.5 %collective-permute-start.11 = (f32[2,1,32,256]{3,2,1,0:T(8,128)S(1)}, f32[2,1,32,256]{3,2,1,0:T(8,128)S(1)}, u32[]{:S(2)}, u32[]{:S(2)}) collective-permute-start(f32[2,1,32,256]{3,2,1,0:T(8,128)S(1)} %get-tuple-element.137), channel_id=1, source_target_pairs={{0,2},{1,3},{4,6},{5,7},{8,10},{9,11},{12,14},{13,15},{16,18},{17,... | collective-permute-start | bytes 196616 | tf_op jit(solution)/shard_map/ppermute | solution.py:22
  73.2 3.5 %collective-permute-start.17 = (f32[4,1,256]{2,0,1:T(4,128)S(1)}, f32[4,1,256]{2,0,1:T(4,128)S(1)}, u32[]{:S(2)}, u32[]{:S(2)}) collective-permute-start(f32[4,1,256]{2,0,1:T(4,128)S(1)} %collective-permute-done.15), channel_id=1, source_target_pairs={{0,13},{1,0},{4,1},{5,4},{8,5},{9,8},{12,9},{13,12},{2,15},{3,2},{... | collective-permute-start | bytes 12296 | tf_op jit(solution)/shard_map/ppermute | solution.py:54
  78.0 3.5 %collective-permute-start.19 = (f32[4,1,256]{2,0,1:T(4,128)S(1)}, f32[4,1,256]{2,0,1:T(4,128)S(1)}, u32[]{:S(2)}, u32[]{:S(2)}) collective-permute-start(f32[4,1,256]{2,0,1:T(4,128)S(1)} %collective-permute-done.17), channel_id=1, source_target_pairs={{0,13},{1,0},{4,1},{5,4},{8,5},{9,8},{12,9},{13,12},{2,15},{3,2},{... | collective-permute-start | bytes 12296 | tf_op jit(solution)/shard_map/ppermute | solution.py:54
  82.9 4.8 %collective-permute-done.20 = f32[4,1,256]{2,0,1:T(4,128)S(1)} collective-permute-done((f32[4,1,256]{2,0,1:T(4,128)S(1)}, f32[4,1,256]{2,0,1:T(4,128)S(1)}, u32[]{:S(2)}, u32[]{:S(2)}) %collective-permute-start.20) | collective-permute-done | bytes 4128 | tf_op jit(solution)/shard_map/ppermute | solution.py:49
  89.1 1.5 collective-permute-start.13
  92.2 1.5 collective-permute-done.21
  93.7 1.9 multiply_reduce_fusion.7
  95.9 3.4 %collective-permute-start.26 = (f32[4,1,256]{2,0,1:T(4,128)S(1)}, f32[4,1,256]{2,0,1:T(4,128)S(1)}, u32[]{:S(2)}, u32[]{:S(2)}) collective-permute-start(f32[4,1,256]{2,0,1:T(4,128)S(1)} %get-tuple-element.145), channel_id=1, source_target_pairs={{0,13},{1,0},{4,1},{5,4},{8,5},{9,8},{12,9},{13,12},{2,15},{3,2},{... | collective-permute-start | bytes 12296 | tf_op jit(solution)/shard_map/ppermute | solution.py:54
  101.3 4.5 %collective-permute-start.22 = (f32[2,1,32,256]{3,2,1,0:T(8,128)S(1)}, f32[2,1,32,256]{3,2,1,0:T(8,128)S(1)}, u32[]{:S(2)}, u32[]{:S(2)}) collective-permute-start(f32[2,1,32,256]{3,2,1,0:T(8,128)S(1)} %get-tuple-element.133), channel_id=1, source_target_pairs={{0,2},{1,3},{4,6},{5,7},{8,10},{9,11},{12,14},{13,15},{16,18},{17,... | collective-permute-start | bytes 196616 | tf_op jit(solution)/shard_map/ppermute | solution.py:22
  107.3 3.5 %collective-permute-start.28 = (f32[4,1,256]{2,0,1:T(4,128)S(1)}, f32[4,1,256]{2,0,1:T(4,128)S(1)}, u32[]{:S(2)}, u32[]{:S(2)}) collective-permute-start(f32[4,1,256]{2,0,1:T(4,128)S(1)} %collective-permute-done.26), channel_id=1, source_target_pairs={{0,13},{1,0},{4,1},{5,4},{8,5},{9,8},{12,9},{13,12},{2,15},{3,2},{... | collective-permute-start | bytes 12296 | tf_op jit(solution)/shard_map/ppermute | solution.py:54
  112.1 3.5 %collective-permute-start.30 = (f32[4,1,256]{2,0,1:T(4,128)S(1)}, f32[4,1,256]{2,0,1:T(4,128)S(1)}, u32[]{:S(2)}, u32[]{:S(2)}) collective-permute-start(f32[4,1,256]{2,0,1:T(4,128)S(1)} %collective-permute-done.28), channel_id=1, source_target_pairs={{0,13},{1,0},{4,1},{5,4},{8,5},{9,8},{12,9},{13,12},{2,15},{3,2},{... | collective-permute-start | bytes 12296 | tf_op jit(solution)/shard_map/ppermute | solution.py:54
  116.9 4.8 %collective-permute-done.31 = f32[4,1,256]{2,0,1:T(4,128)S(1)} collective-permute-done((f32[4,1,256]{2,0,1:T(4,128)S(1)}, f32[4,1,256]{2,0,1:T(4,128)S(1)}, u32[]{:S(2)}, u32[]{:S(2)}) %collective-permute-start.31) | collective-permute-done | bytes 4128 | tf_op jit(solution)/shard_map/ppermute | solution.py:49
  122.0 1.3 gather_fusion.2
  127.2 2.2 fusion.73
  129.4 2.1 fusion.1
  131.5 1.6 copy.271
  133.1 3.1 %reshape.118 = f32[4,1,8192]{2,1,0:T(1,128)} reshape(f32[1024,4,8]{2,1,0:T(4,128)S(1)} %bitcast.197) | data formatting | bytes 262144
  136.2 3.3 %all-to-all-start.2 = ((f32[4,1,8192]{2,1,0:T(1,128)}), f32[4,1,8192]{2,1,0:T(1,128)S(1)}, u32[]{:S(2)}, u32[]{:S(2)}) async-start(f32[4,1,8192]{2,1,0:T(1,128)} %reshape.118), calls=%async_computation.2 | async-start | bytes 262144 | tf_op jit(solution)/shard_map/all_to_all | solution.py:163
  141.4 33.7 %all-reduce.1 = (f32[]{:T(128)}, f32[]{:T(128)}) all-reduce(f32[]{:T(128)S(6)} %add.291, f32[]{:T(128)S(6)} %add.293), channel_id=1, replica_groups=mesh['groups'=2,'pipe'=4,'hour'=2,'seg'=2] {'pipe','hour','seg'}, use_global_device_ids=true, to_apply=%region_5.7 | all-reduce | flops 2 | bytes 16 | tf_op jit(solution)/shard_map/psum | solution.py:193
  176.6 1.6 reduce.1
  178.2 3.4 %reshape.119 = f32[1024,4,8]{2,1,0:T(4,128)S(1)} reshape(f32[4,8192]{1,0:T(4,128)} %reduce.1) | data formatting | bytes 262144
  181.6 1.8 broadcast_multiply_fusion
  183.5 1.9 copy.272
  188.5 3.5 %collective-permute-start.37 = (f32[4,1,256]{2,0,1:T(4,128)S(1)}, f32[4,1,256]{2,0,1:T(4,128)S(1)}, u32[]{:S(2)}, u32[]{:S(2)}) collective-permute-start(f32[4,1,256]{2,0,1:T(4,128)S(1)} %get-tuple-element.143), channel_id=1, source_target_pairs={{0,13},{1,0},{4,1},{5,4},{8,5},{9,8},{12,9},{13,12},{2,15},{3,2},{... | collective-permute-start | bytes 12296 | tf_op jit(solution)/shard_map/ppermute | solution.py:54
  192.1 3.3 %all-to-all-start.3 = ((f32[4,32,256]{2,0,1:T(4,128)}), f32[4,32,256]{2,0,1:T(4,128)S(1)}, u32[]{:S(2)}, u32[]{:S(2)}) async-start(f32[4,32,256]{2,0,1:T(4,128)} %multiply_subtract_fusion.1), calls=%async_computation.3 | async-start | bytes 262144 | tf_op jit(solution)/shard_map/all_to_all | solution.py:181
  197.7 4.5 %collective-permute-start.33 = (f32[2,1,32,256]{3,2,1,0:T(8,128)S(1)}, f32[2,1,32,256]{3,2,1,0:T(8,128)S(1)}, u32[]{:S(2)}, u32[]{:S(2)}) collective-permute-start(f32[2,1,32,256]{3,2,1,0:T(8,128)S(1)} %get-tuple-element.129), channel_id=1, source_target_pairs={{0,2},{1,3},{4,6},{5,7},{8,10},{9,11},{12,14},{13,15},{16,18},{17,... | collective-permute-start | bytes 196616 | tf_op jit(solution)/shard_map/ppermute | solution.py:22
  203.7 3.5 %collective-permute-start.39 = (f32[4,1,256]{2,0,1:T(4,128)S(1)}, f32[4,1,256]{2,0,1:T(4,128)S(1)}, u32[]{:S(2)}, u32[]{:S(2)}) collective-permute-start(f32[4,1,256]{2,0,1:T(4,128)S(1)} %collective-permute-done.37), channel_id=1, source_target_pairs={{0,13},{1,0},{4,1},{5,4},{8,5},{9,8},{12,9},{13,12},{2,15},{3,2},{... | collective-permute-start | bytes 12296 | tf_op jit(solution)/shard_map/ppermute | solution.py:54
  208.5 3.5 %collective-permute-start.41 = (f32[4,1,256]{2,0,1:T(4,128)S(1)}, f32[4,1,256]{2,0,1:T(4,128)S(1)}, u32[]{:S(2)}, u32[]{:S(2)}) collective-permute-start(f32[4,1,256]{2,0,1:T(4,128)S(1)} %collective-permute-done.39), channel_id=1, source_target_pairs={{0,13},{1,0},{4,1},{5,4},{8,5},{9,8},{12,9},{13,12},{2,15},{3,2},{... | collective-permute-start | bytes 12296 | tf_op jit(solution)/shard_map/ppermute | solution.py:54
  213.4 4.8 %collective-permute-done.42 = f32[4,1,256]{2,0,1:T(4,128)S(1)} collective-permute-done((f32[4,1,256]{2,0,1:T(4,128)S(1)}, f32[4,1,256]{2,0,1:T(4,128)S(1)}, u32[]{:S(2)}, u32[]{:S(2)}) %collective-permute-start.42) | collective-permute-done | bytes 4128 | tf_op jit(solution)/shard_map/ppermute | solution.py:49
  220.9 3.0 %collective-permute-start.35 = (f32[2,6,1,256]{1,3,2,0:T(8,128)S(1)}, f32[2,6,1,256]{1,3,2,0:T(8,128)S(1)}, u32[]{:S(2)}, u32[]{:S(2)}) collective-permute-start(f32[2,6,1,256]{1,3,2,0:T(8,128)S(1)} %copy.295), channel_id=1, source_target_pairs={{0,1},{2,3},{4,5},{6,7},{8,9},{10,11},{12,13},{14,15},{16,17},{18,... | collective-permute-start | bytes 36872 | tf_op jit(solution)/shard_map/ppermute | solution.py:22
  225.3 1.8 multiply_reduce_fusion.2
  229.2 2.4 multiply_reduce_fusion.8
  232.9 30.3 %all-reduce = (f32[]{:T(128)}, f32[]{:T(128)}) all-reduce(f32[]{:T(128)S(6)} %add.305, f32[]{:T(128)S(6)} %add.307), channel_id=1, replica_groups=mesh['groups'=2,'pipe'=4,'hour'=2,'seg'=2] {'pipe','hour','seg'}, use_global_device_ids=true, to_apply=%region_12.14 | all-reduce | flops 2 | bytes 16 | tf_op jit(solution)/shard_map/psum | solution.py:193
  (217 shorter events, 47.5 us)
Async XLA Ops:
  1.4 25.7 %collective-permute-start.3 = (f32[4,1,256]{2,1,0:T(1,128)S(1)}, f32[4,1,256]{2,1,0:T(1,128)S(1)}, u32[]{:S(2)}, u32[]{:S(2)}) collective-permute-start(f32[4,1,256]{2,1,0:T(1,128)S(1)} %slice.129), channel_id=1, source_target_pairs={{0,1},{1,4},{4,5},{5,8},{8,9},{9,12},{12,13},{13,0},{2,3},{3,6},{6... | collective-permute-start | bytes 12296 | tf_op jit(solution)/shard_map/ppermute | solution.py:49
  1.8 25.3 %collective-permute-start.4 = (f32[4,1,256]{2,1,0:T(1,128)S(1)}, f32[4,1,256]{2,1,0:T(1,128)S(1)}, u32[]{:S(2)}, u32[]{:S(2)}) collective-permute-start(f32[4,1,256]{2,1,0:T(1,128)S(1)} %slice.129), channel_id=1, source_target_pairs={{0,13},{1,0},{4,1},{5,4},{8,5},{9,8},{12,9},{13,12},{2,15},{3,2},{... | collective-permute-start | bytes 12296 | tf_op jit(solution)/shard_map/ppermute | solution.py:54
  12.1 35.9 %all-to-all-start = ((f32[4,1,8192]{2,1,0:T(1,128)}), f32[4,1,8192]{2,1,0:T(1,128)S(1)}, u32[]{:S(2)}, u32[]{:S(2)}) async-start(f32[4,1,8192]{2,1,0:T(1,128)} %reshape.116), calls=%async_computation | async-start | bytes 262144 | tf_op jit(solution)/shard_map/all_to_all | solution.py:163
  15.6 26.9 %collective-permute-start.1 = (f32[2,1,32,256]{3,2,1,0:T(8,128)S(1)}, f32[2,1,32,256]{3,2,1,0:T(8,128)S(1)}, u32[]{:S(2)}, u32[]{:S(2)}) collective-permute-start(f32[2,1,32,256]{3,2,1,0:T(8,128)S(1)} %get-tuple-element.142), channel_id=1, source_target_pairs={{2,0},{3,1},{6,4},{7,5},{10,8},{11,9},{14,12},{15,13},{18,16},{19,... | collective-permute-start | bytes 196616 | tf_op jit(solution)/shard_map/ppermute | solution.py:24
  16.9 25.6 %collective-permute-start = (f32[2,1,32,256]{3,2,1,0:T(8,128)S(1)}, f32[2,1,32,256]{3,2,1,0:T(8,128)S(1)}, u32[]{:S(2)}, u32[]{:S(2)}) collective-permute-start(f32[2,1,32,256]{3,2,1,0:T(8,128)S(1)} %get-tuple-element.141), channel_id=1, source_target_pairs={{0,2},{1,3},{4,6},{5,7},{8,10},{9,11},{12,14},{13,15},{16,18},{17,... | collective-permute-start | bytes 196616 | tf_op jit(solution)/shard_map/ppermute | solution.py:22
  27.1 4.8 %collective-permute-start.5 = (f32[4,1,256]{2,1,0:T(1,128)S(1)}, f32[4,1,256]{2,1,0:T(1,128)S(1)}, u32[]{:S(2)}, u32[]{:S(2)}) collective-permute-start(f32[4,1,256]{2,1,0:T(1,128)S(1)} %collective-permute-done.3), channel_id=1, source_target_pairs={{0,1},{1,4},{4,5},{5,8},{8,9},{9,12},{12,13},{13,0},{2,3},{3,6},{6... | collective-permute-start | bytes 12296 | tf_op jit(solution)/shard_map/ppermute | solution.py:49
  27.1 4.9 %collective-permute-start.6 = (f32[4,1,256]{2,1,0:T(1,128)S(1)}, f32[4,1,256]{2,1,0:T(1,128)S(1)}, u32[]{:S(2)}, u32[]{:S(2)}) collective-permute-start(f32[4,1,256]{2,1,0:T(1,128)S(1)} %collective-permute-done.4), channel_id=1, source_target_pairs={{0,13},{1,0},{4,1},{5,4},{8,5},{9,8},{12,9},{13,12},{2,15},{3,2},{... | collective-permute-start | bytes 12296 | tf_op jit(solution)/shard_map/ppermute | solution.py:54
  31.9 4.8 %collective-permute-start.7 = (f32[4,1,256]{2,1,0:T(1,128)S(1)}, f32[4,1,256]{2,1,0:T(1,128)S(1)}, u32[]{:S(2)}, u32[]{:S(2)}) collective-permute-start(f32[4,1,256]{2,1,0:T(1,128)S(1)} %collective-permute-done.5), channel_id=1, source_target_pairs={{0,1},{1,4},{4,5},{5,8},{8,9},{9,12},{12,13},{13,0},{2,3},{3,6},{6... | collective-permute-start | bytes 12296 | tf_op jit(solution)/shard_map/ppermute | solution.py:49
  32.0 4.8 %collective-permute-start.8 = (f32[4,1,256]{2,1,0:T(1,128)S(1)}, f32[4,1,256]{2,1,0:T(1,128)S(1)}, u32[]{:S(2)}, u32[]{:S(2)}) collective-permute-start(f32[4,1,256]{2,1,0:T(1,128)S(1)} %collective-permute-done.6), channel_id=1, source_target_pairs={{0,13},{1,0},{4,1},{5,4},{8,5},{9,8},{12,9},{13,12},{2,15},{3,2},{... | collective-permute-start | bytes 12296 | tf_op jit(solution)/shard_map/ppermute | solution.py:54
  36.8 4.8 %collective-permute-start.9 = (f32[4,1,256]{2,1,0:T(1,128)S(1)}, f32[4,1,256]{2,1,0:T(1,128)S(1)}, u32[]{:S(2)}, u32[]{:S(2)}) collective-permute-start(f32[4,1,256]{2,1,0:T(1,128)S(1)} %collective-permute-done.7), channel_id=1, source_target_pairs={{0,1},{1,4},{4,5},{5,8},{8,9},{9,12},{12,13},{13,0},{2,3},{3,6},{6... | collective-permute-start | bytes 12296 | tf_op jit(solution)/shard_map/ppermute | solution.py:49
  42.9 12.9 %collective-permute-start.10 = (f32[2,6,1,256]{3,1,2,0:T(8,128)S(1)}, f32[2,6,1,256]{3,1,2,0:T(8,128)S(1)}, u32[]{:S(2)}, u32[]{:S(2)}) collective-permute-start(f32[2,6,1,256]{3,1,2,0:T(8,128)S(1)} %slice.176), channel_id=1, source_target_pairs={{0,1},{2,3},{4,5},{6,7},{8,9},{10,11},{12,13},{14,15},{16,17},{18,... | collective-permute-start | bytes 36872 | tf_op jit(solution)/shard_map/ppermute | solution.py:22
  44.4 3.4 %collective-permute-start.2 = (f32[2,6,1,256]{1,3,2,0:T(8,128)S(1)}, f32[2,6,1,256]{1,3,2,0:T(8,128)S(1)}, u32[]{:S(2)}, u32[]{:S(2)}) collective-permute-start(f32[2,6,1,256]{1,3,2,0:T(8,128)S(1)} %copy.288), channel_id=1, source_target_pairs={{1,0},{3,2},{5,4},{7,6},{9,8},{11,10},{13,12},{15,14},{17,16},{19,... | collective-permute-start | bytes 36872 | tf_op jit(solution)/shard_map/ppermute | solution.py:24
  57.2 15.9 %collective-permute-start.14 = (f32[4,1,256]{2,0,1:T(4,128)S(1)}, f32[4,1,256]{2,0,1:T(4,128)S(1)}, u32[]{:S(2)}, u32[]{:S(2)}) collective-permute-start(f32[4,1,256]{2,0,1:T(4,128)S(1)} %get-tuple-element.147), channel_id=1, source_target_pairs={{0,1},{1,4},{4,5},{5,8},{8,9},{9,12},{12,13},{13,0},{2,3},{3,6},{6... | collective-permute-start | bytes 12296 | tf_op jit(solution)/shard_map/ppermute | solution.py:49
  57.4 15.8 %collective-permute-start.15 = (f32[4,1,256]{2,0,1:T(4,128)S(1)}, f32[4,1,256]{2,0,1:T(4,128)S(1)}, u32[]{:S(2)}, u32[]{:S(2)}) collective-permute-start(f32[4,1,256]{2,0,1:T(4,128)S(1)} %get-tuple-element.147), channel_id=1, source_target_pairs={{0,13},{1,0},{4,1},{5,4},{8,5},{9,8},{12,9},{13,12},{2,15},{3,2},{... | collective-permute-start | bytes 12296 | tf_op jit(solution)/shard_map/ppermute | solution.py:54
  61.6 65.5 %all-to-all-start.1 = ((f32[4,32,256]{2,0,1:T(4,128)}), f32[4,32,256]{2,0,1:T(4,128)S(1)}, u32[]{:S(2)}, u32[]{:S(2)}) async-start(f32[4,32,256]{2,0,1:T(4,128)} %multiply_subtract_fusion.3), calls=%async_computation.1 | async-start | bytes 262144 | tf_op jit(solution)/shard_map/all_to_all | solution.py:181
  65.9 22.7 %collective-permute-start.12 = (f32[2,1,32,256]{3,2,1,0:T(8,128)S(1)}, f32[2,1,32,256]{3,2,1,0:T(8,128)S(1)}, u32[]{:S(2)}, u32[]{:S(2)}) collective-permute-start(f32[2,1,32,256]{3,2,1,0:T(8,128)S(1)} %get-tuple-element.138), channel_id=1, source_target_pairs={{2,0},{3,1},{6,4},{7,5},{10,8},{11,9},{14,12},{15,13},{18,16},{19,... | collective-permute-start | bytes 196616 | tf_op jit(solution)/shard_map/ppermute | solution.py:24
  67.2 21.4 %collective-permute-start.11 = (f32[2,1,32,256]{3,2,1,0:T(8,128)S(1)}, f32[2,1,32,256]{3,2,1,0:T(8,128)S(1)}, u32[]{:S(2)}, u32[]{:S(2)}) collective-permute-start(f32[2,1,32,256]{3,2,1,0:T(8,128)S(1)} %get-tuple-element.137), channel_id=1, source_target_pairs={{0,2},{1,3},{4,6},{5,7},{8,10},{9,11},{12,14},{13,15},{16,18},{17,... | collective-permute-start | bytes 196616 | tf_op jit(solution)/shard_map/ppermute | solution.py:22
  73.1 4.9 %collective-permute-start.16 = (f32[4,1,256]{2,0,1:T(4,128)S(1)}, f32[4,1,256]{2,0,1:T(4,128)S(1)}, u32[]{:S(2)}, u32[]{:S(2)}) collective-permute-start(f32[4,1,256]{2,0,1:T(4,128)S(1)} %collective-permute-done.14), channel_id=1, source_target_pairs={{0,1},{1,4},{4,5},{5,8},{8,9},{9,12},{12,13},{13,0},{2,3},{3,6},{6... | collective-permute-start | bytes 12296 | tf_op jit(solution)/shard_map/ppermute | solution.py:49
  73.2 4.8 %collective-permute-start.17 = (f32[4,1,256]{2,0,1:T(4,128)S(1)}, f32[4,1,256]{2,0,1:T(4,128)S(1)}, u32[]{:S(2)}, u32[]{:S(2)}) collective-permute-start(f32[4,1,256]{2,0,1:T(4,128)S(1)} %collective-permute-done.15), channel_id=1, source_target_pairs={{0,13},{1,0},{4,1},{5,4},{8,5},{9,8},{12,9},{13,12},{2,15},{3,2},{... | collective-permute-start | bytes 12296 | tf_op jit(solution)/shard_map/ppermute | solution.py:54
  78.0 4.8 %collective-permute-start.18 = (f32[4,1,256]{2,0,1:T(4,128)S(1)}, f32[4,1,256]{2,0,1:T(4,128)S(1)}, u32[]{:S(2)}, u32[]{:S(2)}) collective-permute-start(f32[4,1,256]{2,0,1:T(4,128)S(1)} %collective-permute-done.16), channel_id=1, source_target_pairs={{0,1},{1,4},{4,5},{5,8},{8,9},{9,12},{12,13},{13,0},{2,3},{3,6},{6... | collective-permute-start | bytes 12296 | tf_op jit(solution)/shard_map/ppermute | solution.py:49
  78.0 4.8 %collective-permute-start.19 = (f32[4,1,256]{2,0,1:T(4,128)S(1)}, f32[4,1,256]{2,0,1:T(4,128)S(1)}, u32[]{:S(2)}, u32[]{:S(2)}) collective-permute-start(f32[4,1,256]{2,0,1:T(4,128)S(1)} %collective-permute-done.17), channel_id=1, source_target_pairs={{0,13},{1,0},{4,1},{5,4},{8,5},{9,8},{12,9},{13,12},{2,15},{3,2},{... | collective-permute-start | bytes 12296 | tf_op jit(solution)/shard_map/ppermute | solution.py:54
  82.8 4.8 %collective-permute-start.20 = (f32[4,1,256]{2,0,1:T(4,128)S(1)}, f32[4,1,256]{2,0,1:T(4,128)S(1)}, u32[]{:S(2)}, u32[]{:S(2)}) collective-permute-start(f32[4,1,256]{2,0,1:T(4,128)S(1)} %collective-permute-done.18), channel_id=1, source_target_pairs={{0,1},{1,4},{4,5},{5,8},{8,9},{9,12},{12,13},{13,0},{2,3},{3,6},{6... | collective-permute-start | bytes 12296 | tf_op jit(solution)/shard_map/ppermute | solution.py:49
  89.1 2.8 %collective-permute-start.13 = (f32[2,6,1,256]{1,3,2,0:T(8,128)S(1)}, f32[2,6,1,256]{1,3,2,0:T(8,128)S(1)}, u32[]{:S(2)}, u32[]{:S(2)}) collective-permute-start(f32[2,6,1,256]{1,3,2,0:T(8,128)S(1)} %copy.291), channel_id=1, source_target_pairs={{0,1},{2,3},{4,5},{6,7},{8,9},{10,11},{12,13},{14,15},{16,17},{18,... | collective-permute-start | bytes 36872 | tf_op jit(solution)/shard_map/ppermute | solution.py:22
  90.6 3.1 %collective-permute-start.21 = (f32[2,6,1,256]{3,1,2,0:T(8,128)S(1)}, f32[2,6,1,256]{3,1,2,0:T(8,128)S(1)}, u32[]{:S(2)}, u32[]{:S(2)}) collective-permute-start(f32[2,6,1,256]{3,1,2,0:T(8,128)S(1)} %slice.184), channel_id=1, source_target_pairs={{1,0},{3,2},{5,4},{7,6},{9,8},{11,10},{13,12},{15,14},{17,16},{19,... | collective-permute-start | bytes 36872 | tf_op jit(solution)/shard_map/ppermute | solution.py:24
  95.6 11.5 %collective-permute-start.25 = (f32[4,1,256]{2,0,1:T(4,128)S(1)}, f32[4,1,256]{2,0,1:T(4,128)S(1)}, u32[]{:S(2)}, u32[]{:S(2)}) collective-permute-start(f32[4,1,256]{2,0,1:T(4,128)S(1)} %get-tuple-element.145), channel_id=1, source_target_pairs={{0,1},{1,4},{4,5},{5,8},{8,9},{9,12},{12,13},{13,0},{2,3},{3,6},{6... | collective-permute-start | bytes 12296 | tf_op jit(solution)/shard_map/ppermute | solution.py:49
  95.9 11.4 %collective-permute-start.26 = (f32[4,1,256]{2,0,1:T(4,128)S(1)}, f32[4,1,256]{2,0,1:T(4,128)S(1)}, u32[]{:S(2)}, u32[]{:S(2)}) collective-permute-start(f32[4,1,256]{2,0,1:T(4,128)S(1)} %get-tuple-element.145), channel_id=1, source_target_pairs={{0,13},{1,0},{4,1},{5,4},{8,5},{9,8},{12,9},{13,12},{2,15},{3,2},{... | collective-permute-start | bytes 12296 | tf_op jit(solution)/shard_map/ppermute | solution.py:54
  100.0 23.3 %collective-permute-start.23 = (f32[2,1,32,256]{3,2,1,0:T(8,128)S(1)}, f32[2,1,32,256]{3,2,1,0:T(8,128)S(1)}, u32[]{:S(2)}, u32[]{:S(2)}) collective-permute-start(f32[2,1,32,256]{3,2,1,0:T(8,128)S(1)} %get-tuple-element.134), channel_id=1, source_target_pairs={{2,0},{3,1},{6,4},{7,5},{10,8},{11,9},{14,12},{15,13},{18,16},{19,... | collective-permute-start | bytes 196616 | tf_op jit(solution)/shard_map/ppermute | solution.py:24
  101.3 22.0 %collective-permute-start.22 = (f32[2,1,32,256]{3,2,1,0:T(8,128)S(1)}, f32[2,1,32,256]{3,2,1,0:T(8,128)S(1)}, u32[]{:S(2)}, u32[]{:S(2)}) collective-permute-start(f32[2,1,32,256]{3,2,1,0:T(8,128)S(1)} %get-tuple-element.133), channel_id=1, source_target_pairs={{0,2},{1,3},{4,6},{5,7},{8,10},{9,11},{12,14},{13,15},{16,18},{17,... | collective-permute-start | bytes 196616 | tf_op jit(solution)/shard_map/ppermute | solution.py:22
  107.2 4.9 %collective-permute-start.27 = (f32[4,1,256]{2,0,1:T(4,128)S(1)}, f32[4,1,256]{2,0,1:T(4,128)S(1)}, u32[]{:S(2)}, u32[]{:S(2)}) collective-permute-start(f32[4,1,256]{2,0,1:T(4,128)S(1)} %collective-permute-done.25), channel_id=1, source_target_pairs={{0,1},{1,4},{4,5},{5,8},{8,9},{9,12},{12,13},{13,0},{2,3},{3,6},{6... | collective-permute-start | bytes 12296 | tf_op jit(solution)/shard_map/ppermute | solution.py:49
  107.3 4.8 %collective-permute-start.28 = (f32[4,1,256]{2,0,1:T(4,128)S(1)}, f32[4,1,256]{2,0,1:T(4,128)S(1)}, u32[]{:S(2)}, u32[]{:S(2)}) collective-permute-start(f32[4,1,256]{2,0,1:T(4,128)S(1)} %collective-permute-done.26), channel_id=1, source_target_pairs={{0,13},{1,0},{4,1},{5,4},{8,5},{9,8},{12,9},{13,12},{2,15},{3,2},{... | collective-permute-start | bytes 12296 | tf_op jit(solution)/shard_map/ppermute | solution.py:54
  112.0 4.8 %collective-permute-start.29 = (f32[4,1,256]{2,0,1:T(4,128)S(1)}, f32[4,1,256]{2,0,1:T(4,128)S(1)}, u32[]{:S(2)}, u32[]{:S(2)}) collective-permute-start(f32[4,1,256]{2,0,1:T(4,128)S(1)} %collective-permute-done.27), channel_id=1, source_target_pairs={{0,1},{1,4},{4,5},{5,8},{8,9},{9,12},{12,13},{13,0},{2,3},{3,6},{6... | collective-permute-start | bytes 12296 | tf_op jit(solution)/shard_map/ppermute | solution.py:49
  112.1 4.8 %collective-permute-start.30 = (f32[4,1,256]{2,0,1:T(4,128)S(1)}, f32[4,1,256]{2,0,1:T(4,128)S(1)}, u32[]{:S(2)}, u32[]{:S(2)}) collective-permute-start(f32[4,1,256]{2,0,1:T(4,128)S(1)} %collective-permute-done.28), channel_id=1, source_target_pairs={{0,13},{1,0},{4,1},{5,4},{8,5},{9,8},{12,9},{13,12},{2,15},{3,2},{... | collective-permute-start | bytes 12296 | tf_op jit(solution)/shard_map/ppermute | solution.py:54
  116.9 4.8 %collective-permute-start.31 = (f32[4,1,256]{2,0,1:T(4,128)S(1)}, f32[4,1,256]{2,0,1:T(4,128)S(1)}, u32[]{:S(2)}, u32[]{:S(2)}) collective-permute-start(f32[4,1,256]{2,0,1:T(4,128)S(1)} %collective-permute-done.29), channel_id=1, source_target_pairs={{0,1},{1,4},{4,5},{5,8},{8,9},{9,12},{12,13},{13,0},{2,3},{3,6},{6... | collective-permute-start | bytes 12296 | tf_op jit(solution)/shard_map/ppermute | solution.py:49
  123.6 61.7 %collective-permute-start.32 = (f32[2,6,1,256]{3,1,2,0:T(8,128)S(1)}, f32[2,6,1,256]{3,1,2,0:T(8,128)S(1)}, u32[]{:S(2)}, u32[]{:S(2)}) collective-permute-start(f32[2,6,1,256]{3,1,2,0:T(8,128)S(1)} %slice.192), channel_id=1, source_target_pairs={{0,1},{2,3},{4,5},{6,7},{8,9},{10,11},{12,13},{14,15},{16,17},{18,... | collective-permute-start | bytes 36872 | tf_op jit(solution)/shard_map/ppermute | solution.py:22
  125.8 13.8 %collective-permute-start.24 = (f32[2,6,1,256]{1,3,2,0:T(8,128)}, f32[2,6,1,256]{1,3,2,0:T(8,128)}, u32[]{:S(2)}, u32[]{:S(2)}) collective-permute-start(f32[2,6,1,256]{1,3,2,0:T(8,128)} %copy.292), channel_id=1, source_target_pairs={{1,0},{3,2},{5,4},{7,6},{9,8},{11,10},{13,12},{15,14},{17,16},{19,... | collective-permute-start | bytes 36872 | tf_op jit(solution)/shard_map/ppermute | solution.py:24
  136.2 40.4 %all-to-all-start.2 = ((f32[4,1,8192]{2,1,0:T(1,128)}), f32[4,1,8192]{2,1,0:T(1,128)S(1)}, u32[]{:S(2)}, u32[]{:S(2)}) async-start(f32[4,1,8192]{2,1,0:T(1,128)} %reshape.118), calls=%async_computation.2 | async-start | bytes 262144 | tf_op jit(solution)/shard_map/all_to_all | solution.py:163
  188.5 15.1 %collective-permute-start.36 = (f32[4,1,256]{2,0,1:T(4,128)S(1)}, f32[4,1,256]{2,0,1:T(4,128)S(1)}, u32[]{:S(2)}, u32[]{:S(2)}) collective-permute-start(f32[4,1,256]{2,0,1:T(4,128)S(1)} %get-tuple-element.143), channel_id=1, source_target_pairs={{0,1},{1,4},{4,5},{5,8},{8,9},{9,12},{12,13},{13,0},{2,3},{3,6},{6... | collective-permute-start | bytes 12296 | tf_op jit(solution)/shard_map/ppermute | solution.py:49
  188.5 15.2 %collective-permute-start.37 = (f32[4,1,256]{2,0,1:T(4,128)S(1)}, f32[4,1,256]{2,0,1:T(4,128)S(1)}, u32[]{:S(2)}, u32[]{:S(2)}) collective-permute-start(f32[4,1,256]{2,0,1:T(4,128)S(1)} %get-tuple-element.143), channel_id=1, source_target_pairs={{0,13},{1,0},{4,1},{5,4},{8,5},{9,8},{12,9},{13,12},{2,15},{3,2},{... | collective-permute-start | bytes 12296 | tf_op jit(solution)/shard_map/ppermute | solution.py:54
  192.1 37.0 %all-to-all-start.3 = ((f32[4,32,256]{2,0,1:T(4,128)}), f32[4,32,256]{2,0,1:T(4,128)S(1)}, u32[]{:S(2)}, u32[]{:S(2)}) async-start(f32[4,32,256]{2,0,1:T(4,128)} %multiply_subtract_fusion.1), calls=%async_computation.3 | async-start | bytes 262144 | tf_op jit(solution)/shard_map/all_to_all | solution.py:181
  196.4 22.7 %collective-permute-start.34 = (f32[2,1,32,256]{3,2,1,0:T(8,128)S(1)}, f32[2,1,32,256]{3,2,1,0:T(8,128)S(1)}, u32[]{:S(2)}, u32[]{:S(2)}) collective-permute-start(f32[2,1,32,256]{3,2,1,0:T(8,128)S(1)} %get-tuple-element.130), channel_id=1, source_target_pairs={{2,0},{3,1},{6,4},{7,5},{10,8},{11,9},{14,12},{15,13},{18,16},{19,... | collective-permute-start | bytes 196616 | tf_op jit(solution)/shard_map/ppermute | solution.py:24
  197.7 21.4 %collective-permute-start.33 = (f32[2,1,32,256]{3,2,1,0:T(8,128)S(1)}, f32[2,1,32,256]{3,2,1,0:T(8,128)S(1)}, u32[]{:S(2)}, u32[]{:S(2)}) collective-permute-start(f32[2,1,32,256]{3,2,1,0:T(8,128)S(1)} %get-tuple-element.129), channel_id=1, source_target_pairs={{0,2},{1,3},{4,6},{5,7},{8,10},{9,11},{12,14},{13,15},{16,18},{17,... | collective-permute-start | bytes 196616 | tf_op jit(solution)/shard_map/ppermute | solution.py:22
  203.6 4.9 %collective-permute-start.38 = (f32[4,1,256]{2,0,1:T(4,128)S(1)}, f32[4,1,256]{2,0,1:T(4,128)S(1)}, u32[]{:S(2)}, u32[]{:S(2)}) collective-permute-start(f32[4,1,256]{2,0,1:T(4,128)S(1)} %collective-permute-done.36), channel_id=1, source_target_pairs={{0,1},{1,4},{4,5},{5,8},{8,9},{9,12},{12,13},{13,0},{2,3},{3,6},{6... | collective-permute-start | bytes 12296 | tf_op jit(solution)/shard_map/ppermute | solution.py:49
  203.7 4.8 %collective-permute-start.39 = (f32[4,1,256]{2,0,1:T(4,128)S(1)}, f32[4,1,256]{2,0,1:T(4,128)S(1)}, u32[]{:S(2)}, u32[]{:S(2)}) collective-permute-start(f32[4,1,256]{2,0,1:T(4,128)S(1)} %collective-permute-done.37), channel_id=1, source_target_pairs={{0,13},{1,0},{4,1},{5,4},{8,5},{9,8},{12,9},{13,12},{2,15},{3,2},{... | collective-permute-start | bytes 12296 | tf_op jit(solution)/shard_map/ppermute | solution.py:54
  208.5 4.8 %collective-permute-start.40 = (f32[4,1,256]{2,0,1:T(4,128)S(1)}, f32[4,1,256]{2,0,1:T(4,128)S(1)}, u32[]{:S(2)}, u32[]{:S(2)}) collective-permute-start(f32[4,1,256]{2,0,1:T(4,128)S(1)} %collective-permute-done.38), channel_id=1, source_target_pairs={{0,1},{1,4},{4,5},{5,8},{8,9},{9,12},{12,13},{13,0},{2,3},{3,6},{6... | collective-permute-start | bytes 12296 | tf_op jit(solution)/shard_map/ppermute | solution.py:49
  208.5 4.8 %collective-permute-start.41 = (f32[4,1,256]{2,0,1:T(4,128)S(1)}, f32[4,1,256]{2,0,1:T(4,128)S(1)}, u32[]{:S(2)}, u32[]{:S(2)}) collective-permute-start(f32[4,1,256]{2,0,1:T(4,128)S(1)} %collective-permute-done.39), channel_id=1, source_target_pairs={{0,13},{1,0},{4,1},{5,4},{8,5},{9,8},{12,9},{13,12},{2,15},{3,2},{... | collective-permute-start | bytes 12296 | tf_op jit(solution)/shard_map/ppermute | solution.py:54
  213.3 4.8 %collective-permute-start.42 = (f32[4,1,256]{2,0,1:T(4,128)S(1)}, f32[4,1,256]{2,0,1:T(4,128)S(1)}, u32[]{:S(2)}, u32[]{:S(2)}) collective-permute-start(f32[4,1,256]{2,0,1:T(4,128)S(1)} %collective-permute-done.40), channel_id=1, source_target_pairs={{0,1},{1,4},{4,5},{5,8},{8,9},{9,12},{12,13},{13,0},{2,3},{3,6},{6... | collective-permute-start | bytes 12296 | tf_op jit(solution)/shard_map/ppermute | solution.py:49
  219.5 5.8 %collective-permute-start.43 = (f32[2,6,1,256]{3,1,2,0:T(8,128)S(1)}, f32[2,6,1,256]{3,1,2,0:T(8,128)S(1)}, u32[]{:S(2)}, u32[]{:S(2)}) collective-permute-start(f32[2,6,1,256]{3,1,2,0:T(8,128)S(1)} %slice.200), channel_id=1, source_target_pairs={{1,0},{3,2},{5,4},{7,6},{9,8},{11,10},{13,12},{15,14},{17,16},{19,... | collective-permute-start | bytes 36872 | tf_op jit(solution)/shard_map/ppermute | solution.py:24
  220.9 4.2 %collective-permute-start.35 = (f32[2,6,1,256]{1,3,2,0:T(8,128)S(1)}, f32[2,6,1,256]{1,3,2,0:T(8,128)S(1)}, u32[]{:S(2)}, u32[]{:S(2)}) collective-permute-start(f32[2,6,1,256]{1,3,2,0:T(8,128)S(1)} %copy.295), channel_id=1, source_target_pairs={{0,1},{2,3},{4,5},{6,7},{8,9},{10,11},{12,13},{14,15},{16,17},{18,... | collective-permute-start | bytes 36872 | tf_op jit(solution)/shard_map/ppermute | solution.py:22
  (16 other events, 218.4 us)
